TPU v7x, 256 devices: a whole 4x4x8 slice. The times are simulated.
256 devices in a mesh: row: 32 (over x, y, core), col: 8 (over z).
Axes of the slice: x: 4, y: 4, z: 8, core: 2. Of those that a mesh axis runs over, the one named last changes fastest.
Arguments:
- patches: bfloat16 [16, 256, 6144], P(None, 'col', 'row'), may hold values from -30 to 30
- out_grads: bfloat16 [16, 256, 24576], P(None, 'row', 'col'), may hold values from -8 to 8
Outputs:
- clipped: float32 [6144, 24576], P('row', 'col')
- norms: float32 [16], replicated
All inputs are finite; a program needn't handle non-finite values.
Results may differ from a plain program's by a relative error of at most 0.0003.
Values may be sent and summed in bfloat16 or wider, within the bound.
A program may use at most 128 MiB of HBM per device.

v0:
```python
import math

import jax
import jax.numpy as jnp
from jax import lax
from jax.sharding import PartitionSpec as P

D = 6144
HID = 24576


def image_tile(x_one, g_one):
    return lax.dot_general(
        x_one, g_one, (((0,), (0,)), ((), ())), preferred_element_type=jnp.float32
    )


def shards(patches, out_grads):
    gathered_x = lax.all_gather(patches, "col", axis=1, tiled=True)
    gathered_g = lax.all_gather(out_grads, "row", axis=1, tiled=True)
    gram_in = jnp.einsum("bsd,btd->bst", gathered_x, gathered_x, preferred_element_type=jnp.float32)
    gram_in = lax.psum(gram_in.astype(jnp.bfloat16), "row").astype(jnp.float32)
    gram_out = jnp.einsum(
        "bsh,bth->bst", gathered_g, gathered_g, preferred_element_type=jnp.float32
    )
    gram_out = lax.psum(gram_out.astype(jnp.bfloat16), "col").astype(jnp.float32)
    squares = jnp.sum(gram_in * gram_out, axis=(1, 2))
    norms = jnp.sqrt(squares) / math.sqrt(D * HID)
    scale = 1.0 / jnp.maximum(norms, 1.0)

    def accumulate(total, item):
        x_one, g_one, factor = item
        return (total + factor * image_tile(x_one, g_one), None)

    start_total = jnp.zeros((gathered_x.shape[2], gathered_g.shape[2]), jnp.float32)
    clipped, unused = lax.scan(accumulate, start_total, (gathered_x, gathered_g, scale))
    return (clipped, norms)


def solution(mesh):
    in_specs = (P(None, "col", "row"), P(None, "row", "col"))
    out_specs = (P("row", "col"), P())
    return jax.shard_map(shards, mesh=mesh, in_specs=in_specs, out_specs=out_specs, check_vma=False)
```

profile of v0, /device:TPU:1, one launch (start us, length us, event | category | flops | bytes accessed | tf_op | source)
XLA Modules:
  0.0 423.0 jit_solution(1526754027901264517)
XLA Ops:
  7.2 0.0 all-gather.3.cloned.1.call-start
  7.2 0.7 all-gather.3.cloned.1.call-update
  7.9 0.0 all-gather.5.cloned.1.call-start
  7.9 0.7 all-gather.5.cloned.1.call-update
  8.6 0.0 all-reduce.3.cloned.1.call-start
  8.7 42.4 %all-gather.3.cloned.1.call-done = bf16[16,256,192]{2,1,0:T(8,128)(2,1)} async-done(((bf16[16,32,192]{2,1,0:T(8,128)(2,1)}), bf16[16,256,192]{2,1,0:T(8,128)(2,1)}) %all-gather.3.cloned.1.call-update) | async-done | bytes 1572880 | tf_op jit(solution)/shard_map/all_gather | solution.py:19
  51.0 4.3 %convolution_convert_fusion = bf16[16,256,256]{2,1,0:T(8,128)(2,1)} fusion(bf16[16,256,192]{2,1,0:T(8,128)(2,1)} %all-gather.3.cloned.1.call-done), kind=kOutput, calls=%fused_computation.8 | convolution fusion | flops 403701760 | bytes 3670016 | tf_op jit(solution)/shard_map/bsd,btd->bst/dot_general | solution.py:21
  55.4 0.0 all-reduce.5.cloned.1.call-start
  55.4 98.1 %all-gather.5.cloned.1.call-done = bf16[16,256,3072]{2,1,0:T(8,128)(2,1)} async-done(((bf16[16,8,3072]{2,1,0:T(8,128)(2,1)}), bf16[16,256,3072]{2,1,0:T(8,128)(2,1)}) %all-gather.5.cloned.1.call-update) | async-done | bytes 25165840 | tf_op jit(solution)/shard_map/all_gather | solution.py:20
  153.5 19.7 %convolution_convert_fusion.1 = bf16[16,256,256]{2,1,0:T(8,128)(2,1)} fusion(bf16[16,256,3072]{2,1,0:T(8,128)(2,1)} %all-gather.5.cloned.1.call-done), kind=kOutput, calls=%fused_computation.9 | convolution fusion | flops 6443499520 | bytes 27262976 | tf_op jit(solution)/shard_map/bsh,bth->bst/dot_general | solution.py:23
  173.3 100.1 %all-reduce.3.cloned.1.call-done = bf16[16,256,256]{2,1,0:T(8,128)(2,1)} async-done(((bf16[16,256,256]{2,1,0:T(8,128)(2,1)}), bf16[16,256,256]{2,1,0:T(8,128)(2,1)}) %all-reduce.3.cloned.1.call-update) | async-done | bytes 2097168 | tf_op jit(solution)/shard_map/psum | solution.py:22
  273.3 81.5 %all-reduce.5.cloned.1.call-done = bf16[16,256,256]{2,1,0:T(8,128)(2,1)} async-done(((bf16[16,256,256]{2,1,0:T(8,128)(2,1)}), bf16[16,256,256]{2,1,0:T(8,128)(2,1)}) %all-reduce.5.cloned.1.call-update) | async-done | bytes 2097168 | tf_op jit(solution)/shard_map/psum | solution.py:26
  354.8 2.9 multiply_reduce_fusion
  357.7 0.5 maximum_divide_fusion
  358.2 56.9 %while.11 = (s32[]{:T(128)}, f32[192,3072]{1,0:T(8,128)S(1)}, f32[16]{0:T(128)S(1)}, bf16[16,256,192]{2,1,0:T(8,128)(2,1)}, bf16[16,256,3072]{2,1,0:T(8,128)(2,1)}, /*index=5*/s32[]{:T(128)}, s32[]{:T(128)}) while((s32[]{:T(128)}, f32[192,3072]{1,0:T(8,128)S(1)}, f32[16]{0:T(128)S(1)}, bf16[16,256,192]{2,1,0:T(8,128)(2,1)}, ...), condition=%wide.region_4.5_spmd.clone, body=%wide.region_3.4_spmd.clone.sunk | while | flops 303759360 | bytes 6424163 | solution.py:36
  358.2 0.6 dynamic_slice.28
  358.8 3.0 fusion.15
  361.8 0.6 dynamic_slice.28
  362.4 2.9 fusion.15
  365.3 0.6 dynamic_slice.28
  365.9 2.9 fusion.15
  368.9 0.6 dynamic_slice.28
  369.5 2.9 fusion.15
  372.4 0.6 dynamic_slice.28
  373.0 2.9 fusion.15
  376.0 0.6 dynamic_slice.28
  376.6 2.9 fusion.15
  379.5 0.6 dynamic_slice.28
  380.1 2.9 fusion.15
  383.1 0.6 dynamic_slice.28
  383.7 2.9 fusion.15
  386.6 0.6 dynamic_slice.28
  387.2 2.9 fusion.15
  390.2 0.6 dynamic_slice.28
  390.8 2.9 fusion.15
  393.7 0.6 dynamic_slice.28
  394.3 2.9 fusion.15
  397.3 0.6 dynamic_slice.28
  397.9 2.9 fusion.15
  400.9 0.6 dynamic_slice.28
  401.4 2.9 fusion.15
  404.4 0.6 dynamic_slice.28
  405.0 2.9 fusion.15
  408.0 0.6 dynamic_slice.28
  408.5 2.9 fusion.15
  411.5 0.6 dynamic_slice.28
  412.1 2.9 fusion.15
  415.1 1.4 copy-done
  (4 shorter events, 0.0 us)
Async XLA Ops:
  7.2 43.9 %all-gather.3.cloned.1.call-start = ((), (), s32[]{:S(2)}) async-start(), calls=%async_computation | async-start | bytes 2359296 | tf_op jit(solution)/shard_map/all_gather | solution.py:19
  7.9 145.6 %all-gather.5.cloned.1.call-start = ((), (), s32[]{:S(2)}) async-start(), calls=%async_computation.2 | async-start | bytes 25952256 | tf_op jit(solution)/shard_map/all_gather | solution.py:20
  8.6 264.7 %all-reduce.3.cloned.1.call-start = ((), (), s32[]{:S(2)}) async-start(), calls=%async_computation.1 | async-start | bytes 4194304 | tf_op jit(solution)/shard_map/psum | solution.py:22
  55.4 299.4 %all-reduce.5.cloned.1.call-start = ((), (), s32[]{:S(2)}) async-start(), calls=%async_computation.3 | async-start | bytes 4194304 | tf_op jit(solution)/shard_map/psum | solution.py:26
  415.1 1.4 copy-start
Sparse Core Ops, SparseCore 0:
  9.8 41.2 all-gather.2
  53.6 99.8 all-gather.4
  156.7 116.5 all-reduce.2
  276.1 78.6 all-reduce.4
where the time goes:
time: 426 us; the launch traced here: 423 us
  waiting for transfers between devices  323 us (76%)
  matrix products  71.1 us (17%)
  between operations  13.8 us (3%)
  local copies, waits for them, and re-layouts  10.8 us (3%)
    psum x1, waiting for transfers between devices, shards(): gram_in = lax.psum(gram_in.astype(jnp.bfloat16), 'row').astype(jnp.float32)  100 us
    all_gather x1, waiting for transfers between devices, shards(): gathered_g = lax.all_gather(out_grads, 'row', axis=1, tiled=True)  98.1 us
    psum x1, waiting for transfers between devices, shards(): lax.psum(gram_out.astype(jnp.bfloat16), 'col').astype(jnp.float32)  81.5 us
    dot_general x16, matrix products, image_tile(): lax.dot_general(x_one, g_one, (((0,), (0,)), ((), ())), preferred_element...  47.1 us
    all_gather x1, waiting for transfers between devices, shards(): gathered_x = lax.all_gather(patches, 'col', axis=1, tiled=True)  42.4 us
    dot_general x1, matrix products, shards(): jnp.einsum('bsh,bth->bst', gathered_g, gathered_g, preferred_element_type...  19.7 us
    dynamic_slice x16, local copies, waits for them, and re-layouts, shards(): lax.scan(accumulate, start_total, (gathered_x, gathered_g, scale))  9.38 us
  transfers between devices with their start and end apart: 4, of which 4 were waited for; matrix products, arithmetic and copies ran while one was open for 6% of the time, Pallas kernels for 0%

commit v1 on v0

v1 whole, which is shorter than its diff:
```python
import functools
import math

import jax
import jax.numpy as jnp
from jax import lax
from jax.experimental import pallas as pl
from jax.experimental.pallas import tpu as pltpu
from jax.sharding import PartitionSpec as P

D = 6144
HID = 24576
IMAGES = 16
SEQ = 256
CHUNKS = 8
ROWS = 16
WIDTH = 192
COLS = 3072
HALF = COLS // 2
QUARTER = HALF // 2
TILE = 256
BATCHES = ((0, 1, 2), (3, 4), (5, 6), (7,))
F32 = jnp.float32


def kernel(
    x_ref, g_ref, out_ref, norms_ref,
    gbuf, own, sib, xbuf, xt, tiles, scale, sum_z, sum_y, sum_x,
    local_sem, swap_send, swap_recv, x_send, x_recv,
    ici_send, ici_recv, sib_send, sib_recv,
    z_send, z_recv, y_send, y_recv, w_send, w_recv,
):
    row, z = lax.axis_index("row"), lax.axis_index("col")
    core, y, x = lax.rem(row, 2), lax.rem(row // 2, 4), row // 8

    def at(px, py, pc):
        return {"row": (px * 4 + py) * 2 + pc}

    def up(v, d, n=4):
        return lax.rem(v + d + n, n)

    sibling = at(x, y, 1 - core)
    along_z = [{"col": up(z, d, 8)} for d in range(1, 8)]
    along_yc = [
        (up(y, dy), lax.rem(core + dc, 2))
        for dy in range(4) for dc in range(2) if dy or dc
    ]
    along_x = [up(x, d) for d in range(1, 4)]
    ahead = [at(up(x, 1), y, core), at(up(x, -1), y, core), at(x, up(y, 1), core), at(x, up(y, -1), core)]

    load_g = pltpu.make_async_copy(g_ref, own, local_sem.at[0])
    load_x = pltpu.make_async_copy(x_ref, xbuf.at[z], local_sem.at[1])
    load_g.start()
    load_x.start()

    barrier = pltpu.get_barrier_semaphore()
    peers = along_z + [at(x, py, pc) for py, pc in along_yc] + [at(px, y, core) for px in along_x]
    for peer in peers:
        pl.semaphore_signal(barrier, inc=1, device_id=peer)
    pl.semaphore_wait(barrier, len(peers))

    sends = []

    def send(src, dst, s, r, to, keep=True):
        copy = pltpu.make_async_remote_copy(src, dst, s, r, device_id=to)
        copy.start()
        if keep:
            sends.append(copy)

    def arrived(block, s, r, to):
        pltpu.make_async_remote_copy(block, block, s, r, device_id=to).wait_recv()

    parts = (pl.ds(0, ROWS), pl.ds(ROWS, (CHUNKS - 1) * ROWS))
    for i, rows in enumerate(parts):
        send(g_ref.at[rows], sib.at[rows], swap_send.at[i], swap_recv.at[i], sibling)

    def x_step(s):
        for way, last in ((0, 4), (1, 3)):
            sign = 1 if way == 0 else -1
            if 0 < s <= last:
                block = xbuf.at[up(z, -sign * s, 8)]
                arrived(block, x_send.at[way, s - 1], x_recv.at[way, s - 1], {"col": up(z, sign, 8)})
            if s < last:
                here = up(z, -sign * s, 8)
                src = x_ref if s == 0 else xbuf.at[here]
                send(src, xbuf.at[here], x_send.at[way, s], x_recv.at[way, s], {"col": up(z, sign, 8)})

    def merge(j):
        rows = pl.ds(j * ROWS, ROWS)
        for c in range(0, COLS, 768):
            cols = pl.ds(c, 768)
            a = own[rows, cols].astype(F32)
            b = sib[rows, cols].astype(F32)
            first = jnp.where(core == 0, a[:8], b[8:])
            second = jnp.where(core == 0, b[:8], a[8:])
            both = jnp.concatenate([first, second], axis=0).astype(jnp.bfloat16)
            gbuf[2 * j + core, x, y, :, cols] = both

    def part(b, half, px, py, piece=None):
        start, size = half * HALF, HALF
        if piece is not None:
            start, size = start + piece * QUARTER, QUARTER
        return gbuf.at[b, px, py, :, pl.ds(start, size)]

    everything = slice(None)

    def block(j, half, stage, way, behind):
        b = 2 * j + core
        sign = 1 if way % 2 == 0 else -1
        piece = None if stage % 2 == 0 else way % 2
        if way < 2:
            px, py = up(x, -sign * behind), y
        else:
            px, py = x, up(y, -sign * behind)
        if stage >= 2:
            if half == 0:
                px = everything
            else:
                py = everything
        return part(b, half, px, py, piece)

    def routes(stage):
        for half in range(2):
            along = half if stage < 2 else 1 - half
            for way in (2 * along, 2 * along + 1):
                yield half, way

    def put(j, stage):
        for half, way in routes(stage):
            src = block(j, half, stage, way, stage % 2)
            slot = stage * 4 + way
            send(src, src, ici_send.at[j, slot], ici_recv.at[j, slot], ahead[way])

    def take(j, stage):
        for half, way in routes(stage):
            slot = stage * 4 + way
            arrived(block(j, half, stage, way, 1 + stage % 2), ici_send.at[j, slot], ici_recv.at[j, slot], ahead[way])

    def strip(b, half, d):
        if half == 0:
            return part(b, 0, everything, up(y, d))
        return part(b, 1, up(x, d), everything)

    def share(j, ds):
        for half in range(2):
            for d in ds:
                slot = half * 4 + d
                src = strip(2 * j + core, half, d)
                send(src, src, sib_send.at[j, slot], sib_recv.at[j, slot], sibling)

    def shared(j):
        for half in range(2):
            for d in range(4):
                slot = half * 4 + d
                arrived(strip(2 * j + 1 - core, half, d), sib_send.at[j, slot], sib_recv.at[j, slot], sibling)

    def s0(j):
        put(j, 0)

    def s1(j):
        take(j, 0)
        put(j, 1)

    def s2(j):
        take(j, 1)
        put(j, 2)
        share(j, (0,))

    def s3(j):
        take(j, 2)
        put(j, 3)
        share(j, (1, 3))

    def s4(j):
        take(j, 3)
        share(j, (2,))

    def turn(b, carry):
        xt[b] = xbuf[:, b].reshape(SEQ, WIDTH).astype(F32).T.astype(jnp.bfloat16)
        return carry

    def product(b, cols):
        g = gbuf[b, :, :, :, cols].reshape(SEQ, TILE)
        return jnp.dot(xt[b], g, preferred_element_type=F32)

    def squares(b, slot):
        def body(n, acc):
            cols = pl.ds(pl.multiple_of(n * TILE, TILE), TILE)
            t = product(b, cols)
            if slot is not None:
                tiles[slot, :, cols] = t
            s = (t * t).reshape(WIDTH // 8, 8, TILE).sum(axis=0)
            return acc + s[:, :128] + s[:, 128:]

        acc = lax.fori_loop(0, COLS // TILE, body, jnp.zeros((8, 128), F32))
        return jnp.sum(acc, axis=0, keepdims=True)

    def images(k):
        return [b for j in BATCHES[k] for b in (2 * j, 2 * j + 1)]

    def compute(j):
        k = [i for i, batch in enumerate(BATCHES) if j in batch][0]
        for b in (2 * j, 2 * j + 1):
            slot = b - 14 if k == len(BATCHES) - 1 else None
            n = images(k).index(b)
            sum_z[k, z, n : n + 1, :] = squares(b, slot)
        if j == BATCHES[k][0] and len(images(k)) < 8:
            sum_z[k, z, len(images(k)) :, :] = jnp.zeros((8 - len(images(k)), 128), F32)

    def reduce_z(k):
        mine = sum_z.at[k, z]
        for i, peer in enumerate(along_z):
            send(mine, mine, z_send.at[k, i], z_recv.at[k, z], peer)

    def reduce_y(k):
        for i, peer in enumerate(along_z):
            arrived(sum_z.at[k, peer["col"]], z_send.at[k, i], z_recv.at[k, peer["col"]], peer)
        me = y * 2 + core
        sum_y[k, me] = jnp.sum(sum_z[k], axis=0)
        mine = sum_y.at[k, me]
        for i, (py, pc) in enumerate(along_yc):
            send(mine, mine, y_send.at[k, i], y_recv.at[k, me], at(x, py, pc))

    def reduce_x(k):
        for i, (py, pc) in enumerate(along_yc):
            it = py * 2 + pc
            arrived(sum_y.at[k, it], y_send.at[k, i], y_recv.at[k, it], at(x, py, pc))
        sum_x[k, x] = jnp.sum(sum_y[k], axis=0)
        mine = sum_x.at[k, x]
        for i, px in enumerate(along_x):
            send(mine, mine, w_send.at[k, i], w_recv.at[k, x], at(px, y, core))

    def reduced(k):
        for i, px in enumerate(along_x):
            arrived(sum_x.at[k, px], w_send.at[k, i], w_recv.at[k, px], at(px, y, core))
        total = jnp.sum(jnp.sum(sum_x[k], axis=0), axis=1, keepdims=True)
        norm = jnp.sqrt(total) / math.sqrt(D * HID)
        norm = jnp.broadcast_to(norm, (8, TILE))
        first, count = images(k)[0], len(images(k))
        norms_ref[first : first + count, :] = norm[:count, :128]
        scale[first : first + count, :] = (1.0 / jnp.maximum(norm, 1.0))[:count]

    def accumulate(bs):
        def body(n, carry):
            cols = pl.ds(pl.multiple_of(n * TILE, TILE), TILE)
            acc = out_ref[:, cols] if bs[0] else jnp.zeros((WIDTH, TILE), F32)
            for b in bs:
                acc = acc + scale[b : b + 1, :] * product(b, cols)
            out_ref[:, cols] = acc
            return carry

        lax.fori_loop(0, COLS // TILE, body, 0)

    def finish():
        def body(n, carry):
            cols = pl.ds(pl.multiple_of(n * TILE, TILE), TILE)
            acc = out_ref[:, cols]
            for b in (14, 15):
                acc = acc + scale[b : b + 1, :] * tiles[b - 14, :, cols]
            out_ref[:, cols] = acc
            return carry

        lax.fori_loop(0, COLS // TILE, body, 0)

    x_step(0)
    load_g.wait()
    load_x.wait()
    arrived(sib.at[parts[0]], swap_send.at[0], swap_recv.at[0], sibling)
    merge(0)
    s0(0)
    arrived(sib.at[parts[1]], swap_send.at[1], swap_recv.at[1], sibling)
    merge(1)
    s0(1)
    for j in range(2, CHUNKS):
        merge(j)
    s1(0)
    s2(0)
    s1(1)
    x_step(1)

    for i in range(CHUNKS):
        if i + 2 < CHUNKS:
            s0(i + 2)
        if i + 1 < CHUNKS:
            s2(i + 1)
        if i == 1:
            x_step(3)
        if i == 2:
            x_step(4)
            lax.fori_loop(0, IMAGES, turn, 0)
            shared(0)
            compute(0)
        s3(i)
        if i == 0:
            x_step(2)
        if i + 2 < CHUNKS:
            s1(i + 2)
        if i == 4:
            reduce_y(0)
        if i == 6:
            reduce_y(1)
        s4(i)
        if i >= 2:
            shared(i - 1)
            compute(i - 1)
        if i == 3:
            reduce_z(0)
        if i == 4:
            reduce_x(0)
        if i == 5:
            reduce_z(1)
            reduced(0)
            accumulate((0, 1, 2, 3, 4, 5))
        if i == 6:
            reduce_x(1)
    reduce_z(2)
    reduced(1)
    reduce_y(2)
    accumulate((6, 7, 8, 9))
    reduce_x(2)
    shared(7)
    compute(7)
    reduce_z(3)
    reduced(2)
    accumulate((10, 11, 12, 13))
    reduce_y(3)
    reduce_x(3)
    for copy in sends:
        copy.wait_send()
    reduced(3)
    finish()


def shards(patches, out_grads):
    g = out_grads.reshape(CHUNKS * ROWS, COLS)
    bf16 = jnp.bfloat16
    dma = pltpu.SemaphoreType.DMA
    nb = len(BATCHES)
    clipped, norms = pl.pallas_call(
        kernel,
        out_shape=(
            jax.ShapeDtypeStruct((WIDTH, COLS), F32),
            jax.ShapeDtypeStruct((IMAGES, 128), F32),
        ),
        in_specs=[pl.BlockSpec(memory_space=pl.ANY)] * 2,
        out_specs=(pl.BlockSpec(memory_space=pltpu.VMEM), pl.BlockSpec(memory_space=pltpu.VMEM)),
        scratch_shapes=[
            pltpu.VMEM((IMAGES, 4, 4, ROWS, COLS), bf16),
            pltpu.VMEM((CHUNKS * ROWS, COLS), bf16),
            pltpu.VMEM((CHUNKS * ROWS, COLS), bf16),
            pltpu.VMEM((8, IMAGES, 32, WIDTH), bf16),
            pltpu.VMEM((IMAGES, WIDTH, SEQ), bf16),
            pltpu.VMEM((2, WIDTH, COLS), F32),
            pltpu.VMEM((IMAGES, TILE), F32),
            pltpu.VMEM((nb, 8, 8, 128), F32),
            pltpu.VMEM((nb, 8, 8, 128), F32),
            pltpu.VMEM((nb, 4, 8, 128), F32),
            dma((2,)),
            dma((2,)), dma((2,)),
            dma((2, 4)), dma((2, 4)),
            dma((CHUNKS, 16)), dma((CHUNKS, 16)),
            dma((CHUNKS, 8)), dma((CHUNKS, 8)),
            dma((nb, 7)), dma((nb, 8)),
            dma((nb, 7)), dma((nb, 8)),
            dma((nb, 3)), dma((nb, 4)),
        ],
        compiler_params=pltpu.CompilerParams(
            collective_id=0, has_side_effects=True, vmem_limit_bytes=56 * 1024 * 1024
        ),
    )(patches, g)
    return (clipped, norms[:, 0])


def solution(mesh):
    in_specs = (P(None, "col", "row"), P(None, "row", "col"))
    out_specs = (P("row", "col"), P())
    return jax.shard_map(shards, mesh=mesh, in_specs=in_specs, out_specs=out_specs, check_vma=False)
```

time: 426 us -> 156 us (0.37)
  waiting for transfers between devices: 323 us -> 0 us
  Pallas kernels: 0 us -> 150 us
  matrix products: 71.1 us -> 0 us
  between operations: 13.8 us -> 0.64 us
  local copies, waits for them, and re-layouts: 10.8 us -> 4.62 us
    psum x2 -> x0, waiting for transfers between devices: 182 us -> none  [the longest x1 100 us: shards(): gram_in = lax.psum(gram_in.astype(jnp.bfloat16), 'row').astype(jnp.float32)]
    pallas_call x0 -> x1, Pallas kernels: none -> 150 us  [shards(): pl.pallas_call(kernel, out_shape=(jax.ShapeDtypeStruct((WIDTH, COLS), F32...]
    all_gather x2 -> x0, waiting for transfers between devices: 140 us -> none  [the longest x1 98.1 us: shards(): gathered_g = lax.all_gather(out_grads, 'row', axis=1, tiled=True)]
    dot_general x18 -> x0, matrix products: 71.1 us -> none  [the longest x16 47.1 us: image_tile(): lax.dot_general(x_one, g_one, (((0,), (0,)), ((), ())), preferred_element...]
    dynamic_slice x16 -> x0, local copies, waits for them, and re-layouts: 9.38 us -> none  [shards(): lax.scan(accumulate, start_total, (gathered_x, gathered_g, scale))]
  transfers between devices with their start and end apart: 4 -> 0, of which waited for: 4 -> 0; matrix products, arithmetic and copies ran while one was open for 6% -> 0% of each run, Pallas kernels for 0% -> 0%
where the time goes in v1:
time: 156 us
  Pallas kernels  150 us (96%)
  local copies, waits for them, and re-layouts  4.62 us (3%)
    pallas_call x1, Pallas kernels, shards(): pl.pallas_call(kernel, out_shape=(jax.ShapeDtypeStruct((WIDTH, COLS), F32...  150 us
    unnamed x1, local copies, waits for them, and re-layouts  3.3 us

profile of v1, /device:TPU:1, one launch (start us, length us, event | category | flops | bytes accessed | tf_op | source)
XLA Modules:
  0.0 155.6 jit_solution(5082534369112444742)
XLA Ops:
  0.6 150.4 %shard_map.41 = (f32[192,3072]{1,0:T(8,128)}, f32[16,128]{1,0:T(8,128)}) custom-call(bf16[16,32,192]{2,1,0:T(8,128)(2,1)} %x_ref.1, bf16[128,3072]{1,0:T(8,128)(2,1)} %bitcast.1), custom_call_target="tpu_custom_call" | custom-call | tf_op jit(solution)/shard_map/pallas_call | solution.py:339
  151.0 1.3 slice_reduce_fusion
  152.3 3.3 %copy.5 = f32[192,3072]{1,0:T(8,128)} copy(f32[192,3072]{1,0:T(8,128)} %get-tuple-element.8) | data formatting | bytes 4718592

commit v2 on v1

v2 whole, which is shorter than its diff:
```python
import itertools
import math

import jax
import jax.numpy as jnp
from jax import lax
from jax.experimental import pallas as pl
from jax.experimental.pallas import tpu as pltpu
from jax.sharding import PartitionSpec as P

D = 6144
HID = 24576
IMAGES = 16
SEQ = 256
CHUNKS = 8
ROWS = 16
WIDTH = 192
COLS = 3072
HALF = COLS // 2
QUARTER = HALF // 2
TILE = 256
BATCHES = ((0, 1, 2, 3), (4, 5), (6, 7))
F32 = jnp.float32


def kernel(
    x_ref, g_ref, out_ref, norms_ref,
    gbuf, own, sib, xbuf, xt, xt_first, tiles, scale, sum_zc, sum_xy,
    local_sem, swap_send, swap_recv, x_send, x_recv,
    ici_send, ici_recv, sib_send, sib_recv,
    zc_send, zc_recv, xy_send, xy_recv,
):
    row, z = lax.axis_index("row"), lax.axis_index("col")
    core, y, x = lax.rem(row, 2), lax.rem(row // 2, 4), row // 8

    def at(px, py, pc):
        return {"row": (px * 4 + py) * 2 + pc}

    def up(v, d, n=4):
        return lax.rem(v + d + n, n)

    sibling = at(x, y, 1 - core)
    along_zc = [
        (up(z, dz, 8), lax.rem(core + dc, 2))
        for dz, dc in sorted(itertools.product(range(8), range(2)), key=lambda d: -min(d[0], 8 - d[0]) - d[1])
        if dz or dc
    ]
    along_xy = [
        (up(x, dx), up(y, dy))
        for dx, dy in sorted(itertools.product(range(4), range(4)), key=lambda d: -min(d[0], 4 - d[0]) - min(d[1], 4 - d[1]))
        if dx or dy
    ]
    ahead = [at(up(x, 1), y, core), at(up(x, -1), y, core), at(x, up(y, 1), core), at(x, up(y, -1), core)]

    load_g = pltpu.make_async_copy(g_ref, own, local_sem.at[0])
    load_x = pltpu.make_async_copy(x_ref, xbuf.at[z], local_sem.at[1])
    load_first = pltpu.make_async_copy(g_ref.at[pl.ds(0, ROWS)], gbuf.at[core, x, y], local_sem.at[2])
    load_g.start()
    load_x.start()
    load_first.start()

    barrier = pltpu.get_barrier_semaphore()
    peers = ahead + [{"col": up(z, 1, 8)}, {"col": up(z, -1, 8)}, sibling]
    for peer in peers:
        pl.semaphore_signal(barrier, inc=1, device_id=peer)
    pl.semaphore_wait(barrier, len(peers))

    sends = []

    def send(src, dst, s, r, to, keep=True):
        copy = pltpu.make_async_remote_copy(src, dst, s, r, device_id=to)
        copy.start()
        if keep:
            sends.append(copy)

    def arrived(block, s, r, to):
        pltpu.make_async_remote_copy(block, block, s, r, device_id=to).wait_recv()

    def swap():
        rows = pl.ds(ROWS, (CHUNKS - 1) * ROWS)
        send(g_ref.at[rows], sib.at[rows], swap_send.at[0], swap_recv.at[0], sibling)

    def x_step(s):
        for way, last in ((0, 4), (1, 3)):
            sign = 1 if way == 0 else -1
            if 0 < s <= last:
                block = xbuf.at[up(z, -sign * s, 8)]
                arrived(block, x_send.at[way, s - 1], x_recv.at[way, s - 1], {"col": up(z, sign, 8)})
            if s < last:
                here = up(z, -sign * s, 8)
                src = x_ref if s == 0 else xbuf.at[here]
                send(src, xbuf.at[here], x_send.at[way, s], x_recv.at[way, s], {"col": up(z, sign, 8)})

    def merge(j):
        rows = pl.ds(j * ROWS, ROWS)
        for c in range(0, COLS, 768):
            cols = pl.ds(c, 768)
            a = own[rows, cols].astype(F32)
            b = sib[rows, cols].astype(F32)
            first = jnp.where(core == 0, a[:8], b[8:])
            second = jnp.where(core == 0, b[:8], a[8:])
            both = jnp.concatenate([first, second], axis=0).astype(jnp.bfloat16)
            gbuf[2 * j + core, x, y, :, cols] = both

    def part(b, half, px, py, piece=None):
        start, size = half * HALF, HALF
        if piece is not None:
            start, size = start + piece * QUARTER, QUARTER
        return gbuf.at[b, px, py, :, pl.ds(start, size)]

    everything = slice(None)

    def block(j, half, stage, way, behind):
        b = 2 * j + core
        sign = 1 if way % 2 == 0 else -1
        piece = None if stage % 2 == 0 else way % 2
        if way < 2:
            px, py = up(x, -sign * behind), y
        else:
            px, py = x, up(y, -sign * behind)
        if stage >= 2:
            if half == 0:
                px = everything
            else:
                py = everything
        return part(b, half, px, py, piece)

    def routes(stage):
        for half in range(2):
            along = half if stage < 2 else 1 - half
            for way in (2 * along, 2 * along + 1):
                yield half, way

    def put(j, stage):
        for half, way in routes(stage):
            src = dst = block(j, half, stage, way, stage % 2)
            if j == 0 and stage == 0:
                src = g_ref.at[pl.ds(0, ROWS), pl.ds(half * HALF, HALF)]
            slot = stage * 4 + way
            send(src, dst, ici_send.at[j, slot], ici_recv.at[j, slot], ahead[way])

    def take(j, stage):
        for half, way in routes(stage):
            slot = stage * 4 + way
            arrived(block(j, half, stage, way, 1 + stage % 2), ici_send.at[j, slot], ici_recv.at[j, slot], ahead[way])

    def strip(b, half, d):
        if half == 0:
            return part(b, 0, everything, up(y, d))
        return part(b, 1, up(x, d), everything)

    def share(j, ds):
        for half in range(2):
            for d in ds:
                slot = half * 4 + d
                src = strip(2 * j + core, half, d)
                send(src, src, sib_send.at[j, slot], sib_recv.at[j, slot], sibling)

    def shared(j):
        for half in range(2):
            for d in range(4):
                slot = half * 4 + d
                arrived(strip(2 * j + 1 - core, half, d), sib_send.at[j, slot], sib_recv.at[j, slot], sibling)

    def s0(j):
        put(j, 0)

    def s1(j):
        take(j, 0)
        put(j, 1)

    def s2(j):
        take(j, 1)
        put(j, 2)
        share(j, (0,))

    def s3(j):
        take(j, 2)
        put(j, 3)
        share(j, (1, 3))

    def s4(j):
        take(j, 3)
        share(j, (2,))

    def turn(b, carry):
        xt[b] = xbuf[:, b].reshape(SEQ, WIDTH).astype(F32).T.astype(jnp.bfloat16)
        return carry

    def turn_first():
        for b in range(2):
            halves = xbuf[:, b].reshape(ROWS, 2, 8, WIDTH).astype(F32)
            nothing = jnp.zeros((ROWS, 8, WIDTH), F32)
            for h in range(2):
                pair = [halves[:, h], nothing] if b == 0 else [nothing, halves[:, h]]
                rows = jnp.stack(pair, axis=1).reshape(SEQ, WIDTH)
                xt_first[b, :, h * SEQ : (h + 1) * SEQ] = rows.T.astype(jnp.bfloat16)

    def product(b, cols):
        if isinstance(b, int) and b < 2:
            g = gbuf[0:2, :, :, :, cols].reshape(2 * SEQ, TILE)
            return jnp.dot(xt_first[b], g, preferred_element_type=F32)
        g = gbuf[b, :, :, :, cols].reshape(SEQ, TILE)
        return jnp.dot(xt[b], g, preferred_element_type=F32)

    def squares(b, slot):
        acc = jnp.zeros((8, 128), F32)
        for n in range(0, COLS, TILE):
            cols = pl.ds(n, TILE)
            t = product(b, cols)
            if slot is not None:
                tiles[slot, :, cols] = t
            s = (t * t).reshape(WIDTH // 8, 8, TILE).sum(axis=0)
            acc = acc + s[:, :128] + s[:, 128:]
        return jnp.sum(acc, axis=0, keepdims=True)

    def images(k):
        return [b for j in BATCHES[k] for b in (2 * j, 2 * j + 1)]

    def compute(j):
        k = [i for i, batch in enumerate(BATCHES) if j in batch][0]
        first, last = images(k)[0], k == len(BATCHES) - 1
        me = z * 2 + core
        if 2 * j == first and len(images(k)) < 8:
            sum_zc[k, me] = jnp.zeros((8, 128), F32)

        def one(b, carry):
            sum_zc[k, me, pl.ds(b - first, 1), :] = squares(b, b - first if last else None)
            return carry

        if j == 0:
            one(0, 0)
            one(1, 0)
        else:
            lax.fori_loop(2 * j, 2 * j + 2, one, 0)

    def reduce_zc(k):
        me = z * 2 + core
        mine = sum_zc.at[k, me]
        for i, (pz, pc) in enumerate(along_zc):
            send(mine, mine, zc_send.at[k, i], zc_recv.at[k, me], dict(at(x, y, pc), col=pz))

    def reduce_xy(k):
        for i, (pz, pc) in enumerate(along_zc):
            it = pz * 2 + pc
            arrived(sum_zc.at[k, it], zc_send.at[k, i], zc_recv.at[k, it], dict(at(x, y, pc), col=pz))
        me = x * 4 + y
        sum_xy[k, me] = jnp.sum(sum_zc[k], axis=0)
        mine = sum_xy.at[k, me]
        for i, (px, py) in enumerate(along_xy):
            send(mine, mine, xy_send.at[k, i], xy_recv.at[k, me], at(px, py, core))

    def reduced(k):
        for i, (px, py) in enumerate(along_xy):
            it = px * 4 + py
            arrived(sum_xy.at[k, it], xy_send.at[k, i], xy_recv.at[k, it], at(px, py, core))
        total = jnp.sum(jnp.sum(sum_xy[k], axis=0), axis=1, keepdims=True)
        norm = jnp.sqrt(total) / math.sqrt(D * HID)
        norm = jnp.broadcast_to(norm, (8, TILE))
        first, count = images(k)[0], len(images(k))
        norms_ref[first : first + count, :] = norm[:count, :128]
        scale[first : first + count, :] = (1.0 / jnp.maximum(norm, 1.0))[:count]

    def accumulate(first, count):
        def add(b):
            for n in range(0, COLS, TILE):
                cols = pl.ds(n, TILE)
                acc = scale[pl.ds(b, 1), :] * product(b, cols) + scale[pl.ds(b + 1, 1), :] * product(b + 1, cols)
                out_ref[:, cols] = acc if isinstance(b, int) and b == 0 else out_ref[:, cols] + acc

        def pair(i, carry):
            add(first + 2 * i)
            return carry

        if first == 0:
            add(0)
        lax.fori_loop(1 if first == 0 else 0, count // 2, pair, 0)

    def finish(first, count):
        for n in range(0, COLS, TILE):
            cols = pl.ds(n, TILE)
            acc = out_ref[:, cols]
            for i in range(count):
                acc = acc + scale[first + i : first + i + 1, :] * tiles[i, :, cols]
            out_ref[:, cols] = acc

    marks = [0]

    def flush():
        for copy in sends[: marks[-2] if len(marks) > 1 else 0]:
            if copy is not None:
                copy.wait_send()
        for i in range(marks[-2] if len(marks) > 1 else 0):
            sends[i] = None
        marks.append(len(sends))

    s0(0)
    swap()
    x_step(0)
    load_g.wait()
    load_x.wait()
    load_first.wait()
    rest = pl.ds(ROWS, (CHUNKS - 1) * ROWS)
    arrived(sib.at[rest], swap_send.at[0], swap_recv.at[0], sibling)
    for j in range(1, CHUNKS):
        merge(j)
        s0(j)
    for j in range(CHUNKS):
        s1(j)
        if j == 4:
            x_step(1)
    s2(0)
    s2(1)
    x_step(2)

    for i in range(CHUNKS):
        s3(i)
        if i + 2 < CHUNKS:
            s2(i + 2)
        if i == 0:
            x_step(3)
        if i == 5:
            reduce_xy(0)
        if i == 6:
            reduced(0)
            accumulate(0, 8)
        if i >= 1:
            s4(i - 1)
            if i == 1:
                x_step(4)
                turn_first()
                lax.fori_loop(2, IMAGES, turn, 0)
            shared(i - 1)
            compute(i - 1)
        if i == 4:
            reduce_zc(0)
        if i == 6:
            reduce_zc(1)
        if i == 7:
            reduce_xy(1)
        flush()
    s4(7)
    shared(7)
    compute(7)
    reduce_zc(2)
    reduced(1)
    accumulate(8, 4)
    reduce_xy(2)
    for copy in sends:
        if copy is not None:
            copy.wait_send()
    reduced(2)
    finish(12, 4)


def shards(patches, out_grads):
    g = out_grads.reshape(CHUNKS * ROWS, COLS)
    bf16 = jnp.bfloat16
    dma = pltpu.SemaphoreType.DMA
    nb = len(BATCHES)
    clipped, norms = pl.pallas_call(
        kernel,
        out_shape=(
            jax.ShapeDtypeStruct((WIDTH, COLS), F32),
            jax.ShapeDtypeStruct((IMAGES, 128), F32),
        ),
        in_specs=[pl.BlockSpec(memory_space=pltpu.HBM)] * 2,
        out_specs=(pl.BlockSpec(memory_space=pltpu.VMEM), pl.BlockSpec(memory_space=pltpu.VMEM)),
        scratch_shapes=[
            pltpu.VMEM((IMAGES, 4, 4, ROWS, COLS), bf16),
            pltpu.VMEM((CHUNKS * ROWS, COLS), bf16),
            pltpu.VMEM((CHUNKS * ROWS, COLS), bf16),
            pltpu.VMEM((8, IMAGES, 32, WIDTH), bf16),
            pltpu.VMEM((IMAGES, WIDTH, SEQ), bf16),
            pltpu.VMEM((2, WIDTH, 2 * SEQ), bf16),
            pltpu.VMEM((2 * len(BATCHES[-1]), WIDTH, COLS), F32),
            pltpu.VMEM((IMAGES, TILE), F32),
            pltpu.VMEM((nb, 16, 8, 128), F32),
            pltpu.VMEM((nb, 16, 8, 128), F32),
            dma((3,)),
            dma((1,)), dma((1,)),
            dma((2, 4)), dma((2, 4)),
            dma((CHUNKS, 16)), dma((CHUNKS, 16)),
            dma((CHUNKS, 8)), dma((CHUNKS, 8)),
            dma((nb, 15)), dma((nb, 16)),
            dma((nb, 15)), dma((nb, 16)),
        ],
        compiler_params=pltpu.CompilerParams(
            collective_id=0, has_side_effects=True, vmem_limit_bytes=46 * 1024 * 1024
        ),
    )(patches, g)
    return (clipped, norms[:, 0])


def solution(mesh):
    in_specs = (P(None, "col", "row"), P(None, "row", "col"))
    out_specs = (P("row", "col"), P())
    return jax.shard_map(shards, mesh=mesh, in_specs=in_specs, out_specs=out_specs, check_vma=False)
```

time: 156 us -> 107 us (0.69)
  Pallas kernels: 150 us -> 102 us
    pallas_call x1, Pallas kernels: 150 us -> 102 us  [shards(): pl.pallas_call(kernel, out_shape=(jax.ShapeDtypeStruct((WIDTH, COLS), F32...]
    unnamed x1 -> x5, local copies, waits for them, and re-layouts: 3.3 us -> 3.48 us
where the time goes in v2:
time: 107 us
  Pallas kernels  102 us (95%)
  local copies, waits for them, and re-layouts  4.11 us (4%)
    pallas_call x1, Pallas kernels, shards(): pl.pallas_call(kernel, out_shape=(jax.ShapeDtypeStruct((WIDTH, COLS), F32...  102 us
    unnamed x5, local copies, waits for them, and re-layouts  3.48 us

profile of v2, /device:TPU:1, one launch (start us, length us, event | category | flops | bytes accessed | tf_op | source)
XLA Modules:
  0.0 106.6 jit_solution(15400862518838803896)
XLA Ops:
  0.6 0.0 copy-start
  0.6 1.1 %copy-done = bf16[16,8,3072]{2,1,0:T(8,128)(2,1)S(1)} copy-done((bf16[16,8,3072]{2,1,0:T(8,128)(2,1)S(1)}, bf16[16,8,3072]{2,1,0:T(8,128)(2,1)}, u32[]{:S(2)}) %copy-start) | copy-done | bytes 786456
  1.8 0.0 copy-start.1
  1.8 0.9 copy-done.1
  2.7 101.9 %shard_map.41 = (f32[192,3072]{1,0:T(8,128)S(1)}, f32[16,128]{1,0:T(8,128)S(1)}) custom-call(bf16[16,32,192]{2,1,0:T(8,128)(2,1)S(1)} %copy-done.1, bf16[128,3072]{1,0:T(8,128)(2,1)S(1)} %bitcast.1), custom_call_target="tpu_custom_call" | custom-call | tf_op jit(solution)/shard_map/pallas_call | solution.py:361
  104.6 0.6 slice_reduce_fusion
  105.2 1.4 %copy.5 = f32[192,3072]{1,0:T(8,128)} copy(f32[192,3072]{1,0:T(8,128)S(1)} %get-tuple-element.8) | data formatting | bytes 4718592
Async XLA Ops:
  0.6 1.1 %copy-start = (bf16[16,8,3072]{2,1,0:T(8,128)(2,1)S(1)}, bf16[16,8,3072]{2,1,0:T(8,128)(2,1)}, u32[]{:S(2)}) copy-start(bf16[16,8,3072]{2,1,0:T(8,128)(2,1)} %param.3) | copy-start | bytes 2359300
  1.8 0.9 copy-start.1

commit v3 on v2

--- a/solution.py
+++ b/solution.py
@@ -19,7 +19,7 @@
 HALF = COLS // 2
 QUARTER = HALF // 2
 TILE = 256
-BATCHES = ((0, 1, 2, 3), (4, 5), (6, 7))
+BATCHES = ((0, 1, 2, 3, 4, 5), (6, 7))
 F32 = jnp.float32
 
 
@@ -217,12 +217,10 @@
     def images(k):
         return [b for j in BATCHES[k] for b in (2 * j, 2 * j + 1)]
 
-    def compute(j):
+    def compute(j, which=(0, 1)):
         k = [i for i, batch in enumerate(BATCHES) if j in batch][0]
         first, last = images(k)[0], k == len(BATCHES) - 1
         me = z * 2 + core
-        if 2 * j == first and len(images(k)) < 8:
-            sum_zc[k, me] = jnp.zeros((8, 128), F32)
 
         def one(b, carry):
             sum_zc[k, me, pl.ds(b - first, 1), :] = squares(b, b - first if last else None)
@@ -231,8 +229,10 @@
         if j == 0:
             one(0, 0)
             one(1, 0)
+        elif len(which) == 2:
+            lax.fori_loop(2 * j, 2 * j + 2, one, 0)
         else:
-            lax.fori_loop(2 * j, 2 * j + 2, one, 0)
+            one(2 * j + which[0], 0)
 
     def reduce_zc(k):
         me = z * 2 + core
@@ -256,7 +256,7 @@
             arrived(sum_xy.at[k, it], xy_send.at[k, i], xy_recv.at[k, it], at(px, py, core))
         total = jnp.sum(jnp.sum(sum_xy[k], axis=0), axis=1, keepdims=True)
         norm = jnp.sqrt(total) / math.sqrt(D * HID)
-        norm = jnp.broadcast_to(norm, (8, TILE))
+        norm = jnp.broadcast_to(norm, (16, TILE))
         first, count = images(k)[0], len(images(k))
         norms_ref[first : first + count, :] = norm[:count, :128]
         scale[first : first + count, :] = (1.0 / jnp.maximum(norm, 1.0))[:count]
@@ -297,6 +297,8 @@
     s0(0)
     swap()
     x_step(0)
+    for k in range(len(BATCHES)):
+        sum_zc[k, z * 2 + core] = jnp.zeros((16, 128), F32)
     load_g.wait()
     load_x.wait()
     load_first.wait()
@@ -319,11 +321,6 @@
             s2(i + 2)
         if i == 0:
             x_step(3)
-        if i == 5:
-            reduce_xy(0)
-        if i == 6:
-            reduced(0)
-            accumulate(0, 8)
         if i >= 1:
             s4(i - 1)
             if i == 1:
@@ -332,24 +329,22 @@
                 lax.fori_loop(2, IMAGES, turn, 0)
             shared(i - 1)
             compute(i - 1)
-        if i == 4:
+        if i == 6:
             reduce_zc(0)
-        if i == 6:
-            reduce_zc(1)
-        if i == 7:
-            reduce_xy(1)
         flush()
     s4(7)
+    reduce_xy(0)
+    compute(7, (core,))
     shared(7)
-    compute(7)
-    reduce_zc(2)
-    reduced(1)
-    accumulate(8, 4)
-    reduce_xy(2)
+    compute(7, (1 - core,))
+    reduce_zc(1)
+    reduced(0)
+    accumulate(0, 12)
+    reduce_xy(1)
     for copy in sends:
         if copy is not None:
             copy.wait_send()
-    reduced(2)
+    reduced(1)
     finish(12, 4)
 
 
@@ -375,8 +370,8 @@
             pltpu.VMEM((2, WIDTH, 2 * SEQ), bf16),
             pltpu.VMEM((2 * len(BATCHES[-1]), WIDTH, COLS), F32),
             pltpu.VMEM((IMAGES, TILE), F32),
-            pltpu.VMEM((nb, 16, 8, 128), F32),
-            pltpu.VMEM((nb, 16, 8, 128), F32),
+            pltpu.VMEM((nb, 16, 16, 128), F32),
+            pltpu.VMEM((nb, 16, 16, 128), F32),
             dma((3,)),
             dma((1,)), dma((1,)),
             dma((2, 4)), dma((2, 4)),

time: 107 us -> 102 us (0.953)
  Pallas kernels: 102 us -> 97.4 us
    pallas_call x1, Pallas kernels: 102 us -> 97.4 us  [shards(): pl.pallas_call(kernel, out_shape=(jax.ShapeDtypeStruct((WIDTH, COLS), F32...]
where the time goes in v3:
time: 102 us
  Pallas kernels  97.4 us (95%)
  local copies, waits for them, and re-layouts  4.11 us (4%)
    pallas_call x1, Pallas kernels, shards(): pl.pallas_call(kernel, out_shape=(jax.ShapeDtypeStruct((WIDTH, COLS), F32...  97.4 us
    unnamed x5, local copies, waits for them, and re-layouts  3.48 us

profile of v3, /device:TPU:1, one launch (start us, length us, event | category | flops | bytes accessed | tf_op | source)
XLA Modules:
  0.0 102.2 jit_solution(11023544229158944954)
XLA Ops:
  0.6 0.0 copy-start
  0.6 1.1 %copy-done = bf16[16,8,3072]{2,1,0:T(8,128)(2,1)S(1)} copy-done((bf16[16,8,3072]{2,1,0:T(8,128)(2,1)S(1)}, bf16[16,8,3072]{2,1,0:T(8,128)(2,1)}, u32[]{:S(2)}) %copy-start) | copy-done | bytes 786456
  1.8 0.0 copy-start.1
  1.8 0.9 copy-done.1
  2.7 97.4 %shard_map.41 = (f32[192,3072]{1,0:T(8,128)S(1)}, f32[16,128]{1,0:T(8,128)S(1)}) custom-call(bf16[16,32,192]{2,1,0:T(8,128)(2,1)S(1)} %copy-done.1, bf16[128,3072]{1,0:T(8,128)(2,1)S(1)} %bitcast.1), custom_call_target="tpu_custom_call" | custom-call | tf_op jit(solution)/shard_map/pallas_call | solution.py:356
  100.2 0.6 slice_reduce_fusion
  100.8 1.4 %copy.5 = f32[192,3072]{1,0:T(8,128)} copy(f32[192,3072]{1,0:T(8,128)S(1)} %get-tuple-element.8) | data formatting | bytes 4718592
Async XLA Ops:
  0.6 1.1 %copy-start = (bf16[16,8,3072]{2,1,0:T(8,128)(2,1)S(1)}, bf16[16,8,3072]{2,1,0:T(8,128)(2,1)}, u32[]{:S(2)}) copy-start(bf16[16,8,3072]{2,1,0:T(8,128)(2,1)} %param.3) | copy-start | bytes 2359300
  1.8 0.9 copy-start.1

commit v4 on v3

--- a/solution.py
+++ b/solution.py
@@ -13,22 +13,23 @@
 IMAGES = 16
 SEQ = 256
 CHUNKS = 8
+COARSE = 6
 ROWS = 16
 WIDTH = 192
 COLS = 3072
 HALF = COLS // 2
 QUARTER = HALF // 2
 TILE = 256
-BATCHES = ((0, 1, 2, 3, 4, 5), (6, 7))
+BATCHES = ((0, 1, 2, 3, 4), (5, 6, 7))
 F32 = jnp.float32
 
 
 def kernel(
     x_ref, g_ref, out_ref, norms_ref,
-    gbuf, own, sib, xbuf, xt, xt_first, tiles, scale, sum_zc, sum_xy,
+    gbuf, own, sib, xbuf, xt, xt_first, xt_twin, tiles, scale, sum_zc, sum_xy,
     local_sem, swap_send, swap_recv, x_send, x_recv,
     ici_send, ici_recv, sib_send, sib_recv,
-    zc_send, zc_recv, xy_send, xy_recv,
+    zc_send, zc_recv, xy_send, xy_recv, twin_send, twin_recv,
 ):
     row, z = lax.axis_index("row"), lax.axis_index("col")
     core, y, x = lax.rem(row, 2), lax.rem(row // 2, 4), row // 8
@@ -150,6 +151,11 @@
         return part(b, 1, up(x, d), everything)
 
     def share(j, ds):
+        if j < COARSE:
+            if 2 in ds:
+                src = gbuf.at[2 * j + core]
+                send(src, src, sib_send.at[j, 0], sib_recv.at[j, 0], sibling)
+            return
         for half in range(2):
             for d in ds:
                 slot = half * 4 + d
@@ -157,6 +163,9 @@
                 send(src, src, sib_send.at[j, slot], sib_recv.at[j, slot], sibling)
 
     def shared(j):
+        if j < COARSE:
+            arrived(gbuf.at[2 * j + 1 - core], sib_send.at[j, 0], sib_recv.at[j, 0], sibling)
+            return
         for half in range(2):
             for d in range(4):
                 slot = half * 4 + d
@@ -217,7 +226,7 @@
     def images(k):
         return [b for j in BATCHES[k] for b in (2 * j, 2 * j + 1)]
 
-    def compute(j, which=(0, 1)):
+    def compute(j):
         k = [i for i, batch in enumerate(BATCHES) if j in batch][0]
         first, last = images(k)[0], k == len(BATCHES) - 1
         me = z * 2 + core
@@ -229,10 +238,28 @@
         if j == 0:
             one(0, 0)
             one(1, 0)
-        elif len(which) == 2:
+        else:
             lax.fori_loop(2 * j, 2 * j + 2, one, 0)
-        else:
-            one(2 * j + which[0], 0)
+
+    def compute_last():
+        b = 2 * (CHUNKS - 1) + core
+        arrived(xt_twin, twin_send.at[0], twin_recv.at[0], sibling)
+        acc = jnp.zeros((8, 128), F32)
+        for n in range(0, COLS, TILE):
+            cols = pl.ds(n, TILE)
+            g = gbuf[b, :, :, :, cols].reshape(SEQ, TILE)
+            mine = jnp.dot(xt[b], g, preferred_element_type=F32)
+            twin = jnp.dot(xt_twin[...], g, preferred_element_type=F32)
+            tiles[4 + core, :, cols] = mine
+            s = (mine * mine + twin * twin).reshape(WIDTH // 8, 8, TILE).sum(axis=0)
+            acc = acc + s[:, :128] + s[:, 128:]
+        sum_zc[1, z * 2 + core, pl.ds(4 + core, 1), :] = jnp.sum(acc, axis=0, keepdims=True)
+
+    def tile_last():
+        b = 2 * CHUNKS - 1 - core
+        for n in range(0, COLS, TILE):
+            cols = pl.ds(n, TILE)
+            tiles[5 - core, :, cols] = product(b, cols)
 
     def reduce_zc(k):
         me = z * 2 + core
@@ -321,31 +348,37 @@
             s2(i + 2)
         if i == 0:
             x_step(3)
+        if i == 7:
+            reduce_xy(0)
         if i >= 1:
             s4(i - 1)
-            if i == 1:
-                x_step(4)
-                turn_first()
-                lax.fori_loop(2, IMAGES, turn, 0)
-            shared(i - 1)
-            compute(i - 1)
+        if i == 1:
+            x_step(4)
+            turn_first()
+            lax.fori_loop(2, IMAGES, turn, 0)
+            send(xt.at[2 * CHUNKS - 1 - core], xt_twin, twin_send.at[0], twin_recv.at[0], sibling)
+        if i >= 2:
+            shared(i - 2)
+            compute(i - 2)
         if i == 6:
             reduce_zc(0)
         flush()
+    shared(6)
+    compute(6)
     s4(7)
-    reduce_xy(0)
-    compute(7, (core,))
+    compute_last()
+    reduce_zc(1)
     shared(7)
-    compute(7, (1 - core,))
-    reduce_zc(1)
+    tile_last()
     reduced(0)
-    accumulate(0, 12)
+    accumulate(0, 4)
     reduce_xy(1)
+    accumulate(4, 6)
     for copy in sends:
         if copy is not None:
             copy.wait_send()
     reduced(1)
-    finish(12, 4)
+    finish(10, 6)
 
 
 def shards(patches, out_grads):
@@ -368,6 +401,7 @@
             pltpu.VMEM((8, IMAGES, 32, WIDTH), bf16),
             pltpu.VMEM((IMAGES, WIDTH, SEQ), bf16),
             pltpu.VMEM((2, WIDTH, 2 * SEQ), bf16),
+            pltpu.VMEM((WIDTH, SEQ), bf16),
             pltpu.VMEM((2 * len(BATCHES[-1]), WIDTH, COLS), F32),
             pltpu.VMEM((IMAGES, TILE), F32),
             pltpu.VMEM((nb, 16, 16, 128), F32),
@@ -379,6 +413,7 @@
             dma((CHUNKS, 8)), dma((CHUNKS, 8)),
             dma((nb, 15)), dma((nb, 16)),
             dma((nb, 15)), dma((nb, 16)),
+            dma((1,)), dma((1,)),
         ],
         compiler_params=pltpu.CompilerParams(
             collective_id=0, has_side_effects=True, vmem_limit_bytes=46 * 1024 * 1024

time: 102 us -> 98.8 us (0.969)
  Pallas kernels: 97.4 us -> 93.9 us
    pallas_call x1, Pallas kernels: 97.4 us -> 93.9 us  [shards(): pl.pallas_call(kernel, out_shape=(jax.ShapeDtypeStruct((WIDTH, COLS), F32...]
where the time goes in v4:
time: 98.8 us; the launch traced here: 98.6 us
  Pallas kernels  93.9 us (95%)
  local copies, waits for them, and re-layouts  4.11 us (4%)
    pallas_call x1, Pallas kernels, shards(): pl.pallas_call(kernel, out_shape=(jax.ShapeDtypeStruct((WIDTH, COLS), F32...  93.9 us
    unnamed x5, local copies, waits for them, and re-layouts  3.48 us

profile of v4, /device:TPU:1, one launch (start us, length us, event | category | flops | bytes accessed | tf_op | source)
XLA Modules:
  0.0 98.6 jit_solution(1577165549411815171)
XLA Ops:
  0.6 0.0 copy-start
  0.6 1.1 %copy-done = bf16[16,8,3072]{2,1,0:T(8,128)(2,1)S(1)} copy-done((bf16[16,8,3072]{2,1,0:T(8,128)(2,1)S(1)}, bf16[16,8,3072]{2,1,0:T(8,128)(2,1)}, u32[]{:S(2)}) %copy-start) | copy-done | bytes 786456
  1.8 0.0 copy-start.1
  1.8 0.9 copy-done.1
  2.7 93.9 %shard_map.41 = (f32[192,3072]{1,0:T(8,128)S(1)}, f32[16,128]{1,0:T(8,128)S(1)}) custom-call(bf16[16,32,192]{2,1,0:T(8,128)(2,1)S(1)} %copy-done.1, bf16[128,3072]{1,0:T(8,128)(2,1)S(1)} %bitcast.1), custom_call_target="tpu_custom_call" | custom-call | tf_op jit(solution)/shard_map/pallas_call | solution.py:389
  96.6 0.6 slice_reduce_fusion
  97.2 1.4 %copy.5 = f32[192,3072]{1,0:T(8,128)} copy(f32[192,3072]{1,0:T(8,128)S(1)} %get-tuple-element.8) | data formatting | bytes 4718592
Async XLA Ops:
  0.6 1.1 %copy-start = (bf16[16,8,3072]{2,1,0:T(8,128)(2,1)S(1)}, bf16[16,8,3072]{2,1,0:T(8,128)(2,1)}, u32[]{:S(2)}) copy-start(bf16[16,8,3072]{2,1,0:T(8,128)(2,1)} %param.3) | copy-start | bytes 2359300
  1.8 0.9 copy-start.1

commit v5 on v4

--- a/solution.py
+++ b/solution.py
@@ -261,29 +261,35 @@
             cols = pl.ds(n, TILE)
             tiles[5 - core, :, cols] = product(b, cols)
 
+    def rows_of(k):
+        return 8 if len(images(k)) <= 8 else 16
+
     def reduce_zc(k):
         me = z * 2 + core
-        mine = sum_zc.at[k, me]
+        rows = pl.ds(0, rows_of(k))
+        mine = sum_zc.at[k, me, rows]
         for i, (pz, pc) in enumerate(along_zc):
             send(mine, mine, zc_send.at[k, i], zc_recv.at[k, me], dict(at(x, y, pc), col=pz))
 
     def reduce_xy(k):
+        rows = pl.ds(0, rows_of(k))
         for i, (pz, pc) in enumerate(along_zc):
             it = pz * 2 + pc
-            arrived(sum_zc.at[k, it], zc_send.at[k, i], zc_recv.at[k, it], dict(at(x, y, pc), col=pz))
+            arrived(sum_zc.at[k, it, rows], zc_send.at[k, i], zc_recv.at[k, it], dict(at(x, y, pc), col=pz))
         me = x * 4 + y
-        sum_xy[k, me] = jnp.sum(sum_zc[k], axis=0)
-        mine = sum_xy.at[k, me]
+        sum_xy[k, me, rows] = jnp.sum(sum_zc[k, :, rows], axis=0)
+        mine = sum_xy.at[k, me, rows]
         for i, (px, py) in enumerate(along_xy):
             send(mine, mine, xy_send.at[k, i], xy_recv.at[k, me], at(px, py, core))
 
     def reduced(k):
+        rows = pl.ds(0, rows_of(k))
         for i, (px, py) in enumerate(along_xy):
             it = px * 4 + py
-            arrived(sum_xy.at[k, it], xy_send.at[k, i], xy_recv.at[k, it], at(px, py, core))
-        total = jnp.sum(jnp.sum(sum_xy[k], axis=0), axis=1, keepdims=True)
+            arrived(sum_xy.at[k, it, rows], xy_send.at[k, i], xy_recv.at[k, it], at(px, py, core))
+        total = jnp.sum(jnp.sum(sum_xy[k, :, rows], axis=0), axis=1, keepdims=True)
         norm = jnp.sqrt(total) / math.sqrt(D * HID)
-        norm = jnp.broadcast_to(norm, (16, TILE))
+        norm = jnp.broadcast_to(norm, (rows_of(k), TILE))
         first, count = images(k)[0], len(images(k))
         norms_ref[first : first + count, :] = norm[:count, :128]
         scale[first : first + count, :] = (1.0 / jnp.maximum(norm, 1.0))[:count]
@@ -346,13 +352,13 @@
         s3(i)
         if i + 2 < CHUNKS:
             s2(i + 2)
-        if i == 0:
+        if i == 1:
             x_step(3)
         if i == 7:
             reduce_xy(0)
         if i >= 1:
             s4(i - 1)
-        if i == 1:
+        if i == 2:
             x_step(4)
             turn_first()
             lax.fori_loop(2, IMAGES, turn, 0)

time: 98.8 us -> 97.6 us (0.988)
  Pallas kernels: 93.9 us -> 92.7 us
    pallas_call x1, Pallas kernels: 93.9 us -> 92.7 us  [shards(): pl.pallas_call(kernel, out_shape=(jax.ShapeDtypeStruct((WIDTH, COLS), F32...]
where the time goes in v5:
time: 97.6 us; the launch traced here: 97.5 us
  Pallas kernels  92.7 us (95%)
  local copies, waits for them, and re-layouts  4.11 us (4%)
    pallas_call x1, Pallas kernels, shards(): pl.pallas_call(kernel, out_shape=(jax.ShapeDtypeStruct((WIDTH, COLS), F32...  92.7 us
    unnamed x5, local copies, waits for them, and re-layouts  3.48 us

profile of v5, /device:TPU:1, one launch (start us, length us, event | category | flops | bytes accessed | tf_op | source)
XLA Modules:
  0.0 97.5 jit_solution(3462616459024682803)
XLA Ops:
  0.6 0.0 copy-start
  0.6 1.1 %copy-done = bf16[16,8,3072]{2,1,0:T(8,128)(2,1)S(1)} copy-done((bf16[16,8,3072]{2,1,0:T(8,128)(2,1)S(1)}, bf16[16,8,3072]{2,1,0:T(8,128)(2,1)}, u32[]{:S(2)}) %copy-start) | copy-done | bytes 786456
  1.8 0.0 copy-start.1
  1.8 0.9 copy-done.1
  2.7 92.7 %shard_map.41 = (f32[192,3072]{1,0:T(8,128)S(1)}, f32[16,128]{1,0:T(8,128)S(1)}) custom-call(bf16[16,32,192]{2,1,0:T(8,128)(2,1)S(1)} %copy-done.1, bf16[128,3072]{1,0:T(8,128)(2,1)S(1)} %bitcast.1), custom_call_target="tpu_custom_call" | custom-call | tf_op jit(solution)/shard_map/pallas_call | solution.py:395
  95.5 0.6 slice_reduce_fusion
  96.1 1.4 %copy.5 = f32[192,3072]{1,0:T(8,128)} copy(f32[192,3072]{1,0:T(8,128)S(1)} %get-tuple-element.8) | data formatting | bytes 4718592
Async XLA Ops:
  0.6 1.1 %copy-start = (bf16[16,8,3072]{2,1,0:T(8,128)(2,1)S(1)}, bf16[16,8,3072]{2,1,0:T(8,128)(2,1)}, u32[]{:S(2)}) copy-start(bf16[16,8,3072]{2,1,0:T(8,128)(2,1)} %param.3) | copy-start | bytes 2359300
  1.8 0.9 copy-start.1
